TPU v7x, 512 devices: a whole 4x4x16 slice. The times are simulated.
512 devices in a mesh: gx: 32 (over y, z_hi, x), gy: 16 (over z_lo, core).
Axes of the slice: x: 4, y: 4, z: 16 (z_hi: 2, z_lo: 8; z = z_hi * 8 + z_lo), core: 2. Of those that a mesh axis runs over, the one named last changes fastest.
Arguments:
- e_field: float32 [3, 256, 256, 128], P(None, 'gx', 'gy'), may hold values from -30 to 30
- h_field: float32 [3, 256, 256, 128], P(None, 'gx', 'gy'), may hold values from -30 to 30
- material: int32 [256, 256, 64], P('gx', 'gy'), may hold values from 0 to 3
- permittivity: float32 [4], replicated, may hold values from 1 to 12
- frequencies: float32 [4], replicated, may hold values from 0.6 to 2.4
Outputs:
- e_out: float32 [3, 256, 256, 128], P(None, 'gx', 'gy')
- h_out: float32 [3, 256, 256, 128], P(None, 'gx', 'gy')
- gram: float32 [8, 8], replicated
All inputs are finite; a program needn't handle non-finite values.
Results may differ from a plain program's by a relative error of at most 0.000096.
Values sent between devices are 32-bit elements; how exact they have to be, the bound alone decides.
No kernel may reach another device: no remote copies, remote signals or barrier semaphores. Data moves between devices by JAX's collectives and lax.ppermute only.
A program may use at most 64 MiB of HBM per device.

v0:
```python
import jax
import jax.numpy as jnp
from jax import lax
from jax.sharding import PartitionSpec as P

NZ = 64
SOURCES = 2
FILTERS = 4
MATERIALS = 4
ITERS = 4
TIME_STEP = 0.5


def from_behind(value, axis, steps):
    count = lax.axis_size(axis)
    pairs = [(source, (source + steps) % count) for source in range(count)]
    return lax.ppermute(value, axis, pairs)


def forward_z(field):
    pad = jnp.zeros(field.shape[:-1] + (SOURCES,), field.dtype)
    return jnp.concatenate([field[..., SOURCES:], pad], axis=-1) - field


def backward_z(field):
    pad = jnp.zeros(field.shape[:-1] + (SOURCES,), field.dtype)
    return field - jnp.concatenate([pad, field[..., :-SOURCES]], axis=-1)


def next_values(e_field):
    plane_x = from_behind(e_field[1:3, :1], "gx", -1)
    plane_y = from_behind(jnp.stack([e_field[0][:, :1], e_field[2][:, :1]]), "gy", -1)
    ey_next_x = jnp.concatenate([e_field[1, 1:], plane_x[0]], axis=0)
    ez_next_x = jnp.concatenate([e_field[2, 1:], plane_x[1]], axis=0)
    ex_next_y = jnp.concatenate([e_field[0][:, 1:], plane_y[0]], axis=1)
    ez_next_y = jnp.concatenate([e_field[2][:, 1:], plane_y[1]], axis=1)
    return (ey_next_x, ez_next_x, ex_next_y, ez_next_y)


def prev_values(h_field):
    plane_x = from_behind(h_field[1:3, -1:], "gx", 1)
    plane_y = from_behind(jnp.stack([h_field[0][:, -1:], h_field[2][:, -1:]]), "gy", 1)
    hy_prev_x = jnp.concatenate([plane_x[0], h_field[1, :-1]], axis=0)
    hz_prev_x = jnp.concatenate([plane_x[1], h_field[2, :-1]], axis=0)
    hx_prev_y = jnp.concatenate([plane_y[0], h_field[0][:, :-1]], axis=1)
    hz_prev_y = jnp.concatenate([plane_y[1], h_field[2][:, :-1]], axis=1)
    return (hy_prev_x, hz_prev_x, hx_prev_y, hz_prev_y)


def advance(e_field, h_field, scaled, next_fn, prev_fn):
    e_x, e_y, e_z = (e_field[0], e_field[1], e_field[2])
    ey_next_x, ez_next_x, ex_next_y, ez_next_y = next_fn(e_field)
    curl_x = ez_next_y - e_z - forward_z(e_y)
    curl_y = forward_z(e_x) - (ez_next_x - e_z)
    curl_z = ey_next_x - e_y - (ex_next_y - e_x)
    h_field = h_field - TIME_STEP * jnp.stack([curl_x, curl_y, curl_z])
    h_x, h_y, h_z = (h_field[0], h_field[1], h_field[2])
    hy_prev_x, hz_prev_x, hx_prev_y, hz_prev_y = prev_fn(h_field)
    curl_x = h_z - hz_prev_y - backward_z(h_y)
    curl_y = backward_z(h_x) - (h_z - hz_prev_x)
    curl_z = h_y - hy_prev_x - (h_x - hx_prev_y)
    e_field = jnp.stack([e_x + scaled * curl_x, e_y + scaled * curl_y, e_z + scaled * curl_z])
    return (e_field, h_field)


def body(e_field, h_field, material, permittivity, frequencies):
    onehot = (material[..., None] == jnp.arange(MATERIALS, dtype=jnp.int32)).astype(jnp.float32)
    permit_cell = jnp.sum(onehot * permittivity, axis=-1)
    permit = jnp.repeat(permit_cell, SOURCES, axis=-1)
    scaled = TIME_STEP / permit
    filtered = jnp.zeros((FILTERS,) + e_field.shape, jnp.float32)
    for step in range(ITERS):
        e_field, h_field = advance(e_field, h_field, scaled, next_values, prev_values)
        weights = jnp.cos(frequencies * ((step + 1) * TIME_STEP))
        filtered = filtered + weights[:, None, None, None, None] * e_field[None]
    count = filtered[0].size // SOURCES
    weighted = (filtered * permit[None, None]).reshape(FILTERS, count, SOURCES)
    plain = filtered.reshape(FILTERS, count, SOURCES)
    local = jnp.einsum("kms,lmt->kslt", weighted, plain, precision=lax.Precision.HIGHEST)
    local = local.reshape(FILTERS * SOURCES, FILTERS * SOURCES)
    summed = lax.psum(local, ("gx", "gy"))
    cells = e_field.shape[1] * lax.axis_size("gx") * e_field.shape[2] * lax.axis_size("gy") * NZ
    return (e_field, h_field, summed / cells)


def solution(mesh):
    in_specs = (P(None, "gx", "gy", None), P(None, "gx", "gy", None), P("gx", "gy", None), P(), P())
    out_specs = (P(None, "gx", "gy", None), P(None, "gx", "gy", None), P())
    return jax.shard_map(body, mesh=mesh, in_specs=in_specs, out_specs=out_specs, check_vma=False)
```

profile of v0, /device:TPU:1, one launch (start us, length us, event | category | flops | bytes accessed | tf_op | source)
XLA Modules:
  0.0 369.0 jit_solution(447718432147306307)
XLA Ops:
  1.4 20.9 %collective-permute-start.1 = (f32[2,1,16,128]{3,2,1,0:T(8,128)S(1)}, f32[2,1,16,128]{3,2,1,0:T(8,128)S(1)}, u32[]{:S(2)}, u32[]{:S(2)}) collective-permute-start(f32[2,1,16,128]{3,2,1,0:T(8,128)S(1)} %slice.390), channel_id=1, source_target_pairs={{0,496},{16,0},{32,16},{48,32},{64,48},{80,64},{96,80},{112,96},{1... | collective-permute-start | bytes 49160 | tf_op jit(solution)/shard_map/ppermute | solution.py:17
  23.2 2.9 collective-permute-start
  29.6 14.0 %mul.282 = f32[24576,2]{1,0:T(8,128)} reshape(f32[3,8,16,128]{3,2,1,0:T(8,128)S(1)} %mul.281) | data formatting | bytes 393216 | tf_op jit(solution)/shard_map/mul | solution.py:77
  43.6 7.5 %copy.782 = f32[2,24576]{1,0:T(2,128)S(1)} copy(f32[2,24576]{0,1:T(8,128)} %bitcast.290) | data formatting | bytes 393216 | tf_op jit(solution)/shard_map/mul | solution.py:77
  51.5 2.7 collective-permute-start.2
  57.0 14.7 %collective-permute-done.3 = f32[2,1,16,128]{3,2,1,0:T(8,128)S(1)} collective-permute-done((f32[2,1,16,128]{3,2,1,0:T(8,128)S(1)}, f32[2,1,16,128]{3,2,1,0:T(8,128)S(1)}, u32[]{:S(2)}, u32[]{:S(2)}) %collective-permute-start.3) | collective-permute-done | bytes 16416 | tf_op jit(solution)/shard_map/ppermute | solution.py:17
  76.4 6.3 %collective-permute-start.4 = (f32[2,8,1,128]{3,1,2,0:T(8,128)S(1)}, f32[2,8,1,128]{3,1,2,0:T(8,128)S(1)}, u32[]{:S(2)}, u32[]{:S(2)}) collective-permute-start(f32[2,8,1,128]{3,1,2,0:T(8,128)S(1)} %pad_maximum_fusion.9), channel_id=1, source_target_pairs={{0,15},{1,0},{2,1},{3,2},{4,3},{5,4},{6,5},{7,6},{8,7},{9,8},{10,9... | collective-permute-start | bytes 24584 | tf_op jit(solution)/shard_map/ppermute | solution.py:17
  82.9 14.0 %mul.260 = f32[24576,2]{1,0:T(8,128)} reshape(f32[3,8,16,128]{3,2,1,0:T(8,128)S(1)} %pad_maximum_fusion.1) | data formatting | bytes 393216 | tf_op jit(solution)/shard_map/mul | solution.py:75
  96.9 7.5 %copy.777 = f32[2,24576]{1,0:T(2,128)S(1)} copy(f32[2,24576]{0,1:T(8,128)} %bitcast.291) | data formatting | bytes 393216 | tf_op jit(solution)/shard_map/mul | solution.py:75
  108.5 4.7 %collective-permute-done.6 = f32[2,8,1,128]{3,1,2,0:T(8,128)S(1)} collective-permute-done((f32[2,8,1,128]{3,1,2,0:T(8,128)S(1)}, f32[2,8,1,128]{3,1,2,0:T(8,128)S(1)}, u32[]{:S(2)}, u32[]{:S(2)}) %collective-permute-start.6) | collective-permute-done | bytes 8224 | tf_op jit(solution)/shard_map/ppermute | solution.py:17
  113.2 10.8 %collective-permute-done.7 = f32[2,1,16,128]{3,2,1,0:T(8,128)S(1)} collective-permute-done((f32[2,1,16,128]{3,2,1,0:T(8,128)S(1)}, f32[2,1,16,128]{3,2,1,0:T(8,128)S(1)}, u32[]{:S(2)}, u32[]{:S(2)}) %collective-permute-start.7) | collective-permute-done | bytes 16416 | tf_op jit(solution)/shard_map/ppermute | solution.py:17
  124.2 4.1 %collective-permute-start.9 = (f32[2,1,16,128]{3,2,1,0:T(8,128)S(1)}, f32[2,1,16,128]{3,2,1,0:T(8,128)S(1)}, u32[]{:S(2)}, u32[]{:S(2)}) collective-permute-start(f32[2,1,16,128]{3,2,1,0:T(8,128)S(1)} %pad_maximum_fusion.5), channel_id=1, source_target_pairs={{0,496},{16,0},{32,16},{48,32},{64,48},{80,64},{96,80},{112,96},{1... | collective-permute-start | bytes 49160 | tf_op jit(solution)/shard_map/ppermute | solution.py:17
  129.2 11.8 %collective-permute-start.8 = (f32[2,8,1,128]{3,1,2,0:T(8,128)S(1)}, f32[2,8,1,128]{3,1,2,0:T(8,128)S(1)}, u32[]{:S(2)}, u32[]{:S(2)}) collective-permute-start(f32[2,8,1,128]{3,1,2,0:T(8,128)S(1)} %pad_maximum_fusion.11), channel_id=1, source_target_pairs={{0,15},{1,0},{2,1},{3,2},{4,3},{5,4},{6,5},{7,6},{8,7},{9,8},{10,9... | collective-permute-start | bytes 24584 | tf_op jit(solution)/shard_map/ppermute | solution.py:17
  141.1 14.0 %mul.265 = f32[24576,2]{1,0:T(8,128)} reshape(f32[3,8,16,128]{3,2,1,0:T(8,128)S(1)} %pad_maximum_fusion.2) | data formatting | bytes 393216 | tf_op jit(solution)/shard_map/mul | solution.py:75
  155.1 7.5 %copy.778 = f32[2,24576]{1,0:T(2,128)S(1)} copy(f32[2,24576]{0,1:T(8,128)} %bitcast.292) | data formatting | bytes 393216 | tf_op jit(solution)/shard_map/mul | solution.py:75
  169.5 13.3 %collective-permute-done.11 = f32[2,1,16,128]{3,2,1,0:T(8,128)S(1)} collective-permute-done((f32[2,1,16,128]{3,2,1,0:T(8,128)S(1)}, f32[2,1,16,128]{3,2,1,0:T(8,128)S(1)}, u32[]{:S(2)}, u32[]{:S(2)}) %collective-permute-start.11) | collective-permute-done | bytes 16416 | tf_op jit(solution)/shard_map/ppermute | solution.py:17
  183.0 3.4 collective-permute-start.13
  187.6 9.7 %collective-permute-start.12 = (f32[2,8,1,128]{3,1,2,0:T(8,128)S(1)}, f32[2,8,1,128]{3,1,2,0:T(8,128)S(1)}, u32[]{:S(2)}, u32[]{:S(2)}) collective-permute-start(f32[2,8,1,128]{3,1,2,0:T(8,128)S(1)} %pad_maximum_fusion.13), channel_id=1, source_target_pairs={{0,15},{1,0},{2,1},{3,2},{4,3},{5,4},{6,5},{7,6},{8,7},{9,8},{10,9... | collective-permute-start | bytes 24584 | tf_op jit(solution)/shard_map/ppermute | solution.py:17
  197.4 14.0 %mul.271 = f32[24576,2]{1,0:T(8,128)} reshape(f32[3,8,16,128]{3,2,1,0:T(8,128)S(1)} %pad_maximum_fusion.3) | data formatting | bytes 393216 | tf_op jit(solution)/shard_map/mul | solution.py:75
  211.4 7.5 %copy.779 = f32[2,24576]{1,0:T(2,128)S(1)} copy(f32[2,24576]{0,1:T(8,128)} %bitcast.293) | data formatting | bytes 393216 | tf_op jit(solution)/shard_map/mul | solution.py:75
  225.8 13.4 %collective-permute-done.15 = f32[2,1,16,128]{3,2,1,0:T(8,128)S(1)} collective-permute-done((f32[2,1,16,128]{3,2,1,0:T(8,128)S(1)}, f32[2,1,16,128]{3,2,1,0:T(8,128)S(1)}, u32[]{:S(2)}, u32[]{:S(2)}) %collective-permute-start.15) | collective-permute-done | bytes 16416 | tf_op jit(solution)/shard_map/ppermute | solution.py:17
  239.3 14.0 %mul.277 = f32[24576,2]{1,0:T(8,128)} reshape(f32[3,8,16,128]{3,2,1,0:T(8,128)S(1)} %pad_maximum_fusion) | data formatting | bytes 393216 | tf_op jit(solution)/shard_map/mul | solution.py:75
  253.3 7.5 %copy.780 = f32[2,24576]{1,0:T(2,128)S(1)} copy(f32[2,24576]{0,1:T(8,128)} %bitcast.294) | data formatting | bytes 393216 | tf_op jit(solution)/shard_map/mul | solution.py:75
  264.8 103.5 %psum.7 = f32[8,8]{1,0:T(8,128)S(1)} all-reduce(f32[8,8]{1,0:T(8,128)S(1)} %fusion.85), channel_id=1, replica_groups=mesh['gx'=32,'gy'=16] {'gx','gy'}, use_global_device_ids=true, to_apply=%region_1.0 | all-reduce | flops 64 | bytes 512 | tf_op jit(solution)/shard_map/psum | solution.py:81
  (153 shorter events, 37.5 us)
Async XLA Ops:
  1.4 49.8 %collective-permute-start.1 = (f32[2,1,16,128]{3,2,1,0:T(8,128)S(1)}, f32[2,1,16,128]{3,2,1,0:T(8,128)S(1)}, u32[]{:S(2)}, u32[]{:S(2)}) collective-permute-start(f32[2,1,16,128]{3,2,1,0:T(8,128)S(1)} %slice.390), channel_id=1, source_target_pairs={{0,496},{16,0},{32,16},{48,32},{64,48},{80,64},{96,80},{112,96},{1... | collective-permute-start | bytes 49160 | tf_op jit(solution)/shard_map/ppermute | solution.py:17
  23.2 28.0 %collective-permute-start = (f32[2,8,1,128]{3,1,2,0:T(8,128)S(1)}, f32[2,8,1,128]{3,1,2,0:T(8,128)S(1)}, u32[]{:S(2)}, u32[]{:S(2)}) collective-permute-start(f32[2,8,1,128]{3,1,2,0:T(8,128)S(1)} %pad_maximum_fusion.7), channel_id=1, source_target_pairs={{0,15},{1,0},{2,1},{3,2},{4,3},{5,4},{6,5},{7,6},{8,7},{9,8},{10,9... | collective-permute-start | bytes 24584 | tf_op jit(solution)/shard_map/ppermute | solution.py:17
  29.6 21.6 %copy-start = (f32[3,8,16,128]{3,2,1,0:T(8,128)S(1)}, f32[3,8,16,128]{3,2,1,0:T(8,128)}, u32[]{:S(2)}) copy-start(f32[3,8,16,128]{3,2,1,0:T(8,128)} %param.5) | copy-start | bytes 589828
  29.6 21.8 %copy-start.2 = (f32[3,8,16,128]{3,2,1,0:T(8,128)S(1)}, f32[3,8,16,128]{3,2,1,0:T(8,128)}, u32[]{:S(2)}) copy-start(f32[3,8,16,128]{3,2,1,0:T(8,128)} %param.6) | copy-start | bytes 589828
  51.5 5.5 %collective-permute-start.2 = (f32[2,8,1,128]{3,1,2,0:T(8,128)S(1)}, f32[2,8,1,128]{3,1,2,0:T(8,128)S(1)}, u32[]{:S(2)}, u32[]{:S(2)}) collective-permute-start(f32[2,8,1,128]{3,1,2,0:T(8,128)S(1)} %pad_maximum_fusion.8), channel_id=1, source_target_pairs={{0,1},{1,2},{2,3},{3,4},{4,5},{5,6},{6,7},{7,8},{8,9},{9,10},{10,1... | collective-permute-start | bytes 24584 | tf_op jit(solution)/shard_map/ppermute | solution.py:17
  54.2 17.4 %collective-permute-start.3 = (f32[2,1,16,128]{3,2,1,0:T(8,128)S(1)}, f32[2,1,16,128]{3,2,1,0:T(8,128)S(1)}, u32[]{:S(2)}, u32[]{:S(2)}) collective-permute-start(f32[2,1,16,128]{3,2,1,0:T(8,128)S(1)} %slice.517), channel_id=1, source_target_pairs={{0,16},{16,32},{32,48},{48,64},{64,80},{80,96},{96,112},{112,128},... | collective-permute-start | bytes 49160 | tf_op jit(solution)/shard_map/ppermute | solution.py:17
  71.8 4.5 %collective-permute-start.5 = (f32[2,1,16,128]{3,2,1,0:T(8,128)S(1)}, f32[2,1,16,128]{3,2,1,0:T(8,128)S(1)}, u32[]{:S(2)}, u32[]{:S(2)}) collective-permute-start(f32[2,1,16,128]{3,2,1,0:T(8,128)S(1)} %pad_maximum_fusion.6), channel_id=1, source_target_pairs={{0,496},{16,0},{32,16},{48,32},{64,48},{80,64},{96,80},{112,96},{1... | collective-permute-start | bytes 49160 | tf_op jit(solution)/shard_map/ppermute | solution.py:17
  76.4 28.0 %collective-permute-start.4 = (f32[2,8,1,128]{3,1,2,0:T(8,128)S(1)}, f32[2,8,1,128]{3,1,2,0:T(8,128)S(1)}, u32[]{:S(2)}, u32[]{:S(2)}) collective-permute-start(f32[2,8,1,128]{3,1,2,0:T(8,128)S(1)} %pad_maximum_fusion.9), channel_id=1, source_target_pairs={{0,15},{1,0},{2,1},{3,2},{4,3},{5,4},{6,5},{7,6},{8,7},{9,8},{10,9... | collective-permute-start | bytes 24584 | tf_op jit(solution)/shard_map/ppermute | solution.py:17
  104.6 8.6 %collective-permute-start.6 = (f32[2,8,1,128]{3,1,2,0:T(8,128)S(1)}, f32[2,8,1,128]{3,1,2,0:T(8,128)S(1)}, u32[]{:S(2)}, u32[]{:S(2)}) collective-permute-start(f32[2,8,1,128]{3,1,2,0:T(8,128)S(1)} %pad_maximum_fusion.10), channel_id=1, source_target_pairs={{0,1},{1,2},{2,3},{3,4},{4,5},{5,6},{6,7},{7,8},{8,9},{9,10},{10,1... | collective-permute-start | bytes 24584 | tf_op jit(solution)/shard_map/ppermute | solution.py:17
  106.6 17.4 %collective-permute-start.7 = (f32[2,1,16,128]{3,2,1,0:T(8,128)S(1)}, f32[2,1,16,128]{3,2,1,0:T(8,128)S(1)}, u32[]{:S(2)}, u32[]{:S(2)}) collective-permute-start(f32[2,1,16,128]{3,2,1,0:T(8,128)S(1)} %slice.545), channel_id=1, source_target_pairs={{0,16},{16,32},{32,48},{48,64},{64,80},{80,96},{96,112},{112,128},... | collective-permute-start | bytes 49160 | tf_op jit(solution)/shard_map/ppermute | solution.py:17
  124.2 5.0 %collective-permute-start.9 = (f32[2,1,16,128]{3,2,1,0:T(8,128)S(1)}, f32[2,1,16,128]{3,2,1,0:T(8,128)S(1)}, u32[]{:S(2)}, u32[]{:S(2)}) collective-permute-start(f32[2,1,16,128]{3,2,1,0:T(8,128)S(1)} %pad_maximum_fusion.5), channel_id=1, source_target_pairs={{0,496},{16,0},{32,16},{48,32},{64,48},{80,64},{96,80},{112,96},{1... | collective-permute-start | bytes 49160 | tf_op jit(solution)/shard_map/ppermute | solution.py:17
  129.2 33.5 %collective-permute-start.8 = (f32[2,8,1,128]{3,1,2,0:T(8,128)S(1)}, f32[2,8,1,128]{3,1,2,0:T(8,128)S(1)}, u32[]{:S(2)}, u32[]{:S(2)}) collective-permute-start(f32[2,8,1,128]{3,1,2,0:T(8,128)S(1)} %pad_maximum_fusion.11), channel_id=1, source_target_pairs={{0,15},{1,0},{2,1},{3,2},{4,3},{5,4},{6,5},{7,6},{8,7},{9,8},{10,9... | collective-permute-start | bytes 24584 | tf_op jit(solution)/shard_map/ppermute | solution.py:17
  162.9 6.6 %collective-permute-start.10 = (f32[2,8,1,128]{3,1,2,0:T(8,128)S(1)}, f32[2,8,1,128]{3,1,2,0:T(8,128)S(1)}, u32[]{:S(2)}, u32[]{:S(2)}) collective-permute-start(f32[2,8,1,128]{3,1,2,0:T(8,128)S(1)} %pad_maximum_fusion.12), channel_id=1, source_target_pairs={{0,1},{1,2},{2,3},{3,4},{4,5},{5,6},{6,7},{7,8},{8,9},{9,10},{10,1... | collective-permute-start | bytes 24584 | tf_op jit(solution)/shard_map/ppermute | solution.py:17
  164.9 18.0 %collective-permute-start.11 = (f32[2,1,16,128]{3,2,1,0:T(8,128)S(1)}, f32[2,1,16,128]{3,2,1,0:T(8,128)S(1)}, u32[]{:S(2)}, u32[]{:S(2)}) collective-permute-start(f32[2,1,16,128]{3,2,1,0:T(8,128)S(1)} %slice.573), channel_id=1, source_target_pairs={{0,16},{16,32},{32,48},{48,64},{64,80},{80,96},{96,112},{112,128},... | collective-permute-start | bytes 49160 | tf_op jit(solution)/shard_map/ppermute | solution.py:17
  183.0 4.5 %collective-permute-start.13 = (f32[2,1,16,128]{3,2,1,0:T(8,128)S(1)}, f32[2,1,16,128]{3,2,1,0:T(8,128)S(1)}, u32[]{:S(2)}, u32[]{:S(2)}) collective-permute-start(f32[2,1,16,128]{3,2,1,0:T(8,128)S(1)} %pad_maximum_fusion.4), channel_id=1, source_target_pairs={{0,496},{16,0},{32,16},{48,32},{64,48},{80,64},{96,80},{112,96},{1... | collective-permute-start | bytes 49160 | tf_op jit(solution)/shard_map/ppermute | solution.py:17
  187.6 31.4 %collective-permute-start.12 = (f32[2,8,1,128]{3,1,2,0:T(8,128)S(1)}, f32[2,8,1,128]{3,1,2,0:T(8,128)S(1)}, u32[]{:S(2)}, u32[]{:S(2)}) collective-permute-start(f32[2,8,1,128]{3,1,2,0:T(8,128)S(1)} %pad_maximum_fusion.13), channel_id=1, source_target_pairs={{0,15},{1,0},{2,1},{3,2},{4,3},{5,4},{6,5},{7,6},{8,7},{9,8},{10,9... | collective-permute-start | bytes 24584 | tf_op jit(solution)/shard_map/ppermute | solution.py:17
  219.1 41.8 %copy-start.1 = (f32[3,8,16,128]{3,2,1,0:T(8,128)}, f32[3,8,16,128]{3,2,1,0:T(8,128)S(1)}, u32[]{:S(2)}) copy-start(f32[3,8,16,128]{3,2,1,0:T(8,128)S(1)} %fusion.3) | copy-start | bytes 589828
  219.2 6.6 %collective-permute-start.14 = (f32[2,8,1,128]{3,1,2,0:T(8,128)S(1)}, f32[2,8,1,128]{3,1,2,0:T(8,128)S(1)}, u32[]{:S(2)}, u32[]{:S(2)}) collective-permute-start(f32[2,8,1,128]{3,1,2,0:T(8,128)S(1)} %pad_maximum_fusion.14), channel_id=1, source_target_pairs={{0,1},{1,2},{2,3},{3,4},{4,5},{5,6},{6,7},{7,8},{8,9},{9,10},{10,1... | collective-permute-start | bytes 24584 | tf_op jit(solution)/shard_map/ppermute | solution.py:17
  221.2 18.0 %collective-permute-start.15 = (f32[2,1,16,128]{3,2,1,0:T(8,128)S(1)}, f32[2,1,16,128]{3,2,1,0:T(8,128)S(1)}, u32[]{:S(2)}, u32[]{:S(2)}) collective-permute-start(f32[2,1,16,128]{3,2,1,0:T(8,128)S(1)} %slice.602), channel_id=1, source_target_pairs={{0,16},{16,32},{32,48},{48,64},{64,80},{80,96},{96,112},{112,128},... | collective-permute-start | bytes 49160 | tf_op jit(solution)/shard_map/ppermute | solution.py:17
  239.3 21.6 %copy-start.3 = (f32[3,8,16,128]{3,2,1,0:T(8,128)}, f32[3,8,16,128]{3,2,1,0:T(8,128)S(1)}, u32[]{:S(2)}) copy-start(f32[3,8,16,128]{3,2,1,0:T(8,128)S(1)} %pad_maximum_fusion) | copy-start | bytes 589828
where the time goes:
time: 370 us; the launch traced here: 369 us
  local copies, waits for them, and re-layouts  113 us (31%)
  blocking collectives  104 us (28%)
  starting transfers between devices  77.3 us (21%)
  waiting for transfers between devices  67.1 us (18%)
  other arithmetic  4.46 us (1%)
    psum x1, blocking collectives, body(): summed = lax.psum(local, ('gx', 'gy'))  104 us
    mul x8, local copies, waits for them, and re-layouts, body(): filtered = filtered + weights[:, None, None, None, None] * e_field[None]  86.2 us
    ppermute x16, starting transfers between devices, from_behind(): return lax.ppermute(value, axis, pairs)  77.3 us
    ppermute x16, waiting for transfers between devices, from_behind(): return lax.ppermute(value, axis, pairs)  67.1 us
    mul x4, local copies, waits for them, and re-layouts, body(): weighted = (filtered * permit[None, None]).reshape(FILTERS, count, SOURCES)  22.1 us
  transfers between devices with their start and end apart: 16, of which 11 were waited for; matrix products, arithmetic and copies ran while one was open for 25% of the time, Pallas kernels for 0%

commit v1 on v0

--- a/solution.py
+++ b/solution.py
@@ -64,6 +64,10 @@
 
 
 def body(e_field, h_field, material, permittivity, frequencies):
+
+    def render_node_over_axis(in_array, a_name):
+        return jnp.sum(lax.all_gather(in_array, axis_name=a_name), 0)
+
     onehot = (material[..., None] == jnp.arange(MATERIALS, dtype=jnp.int32)).astype(jnp.float32)
     permit_cell = jnp.sum(onehot * permittivity, axis=-1)
     permit = jnp.repeat(permit_cell, SOURCES, axis=-1)
@@ -78,7 +82,7 @@
     plain = filtered.reshape(FILTERS, count, SOURCES)
     local = jnp.einsum("kms,lmt->kslt", weighted, plain, precision=lax.Precision.HIGHEST)
     local = local.reshape(FILTERS * SOURCES, FILTERS * SOURCES)
-    summed = lax.psum(local, ("gx", "gy"))
+    summed = render_node_over_axis(local, ("gx", "gy"))
     cells = e_field.shape[1] * lax.axis_size("gx") * e_field.shape[2] * lax.axis_size("gy") * NZ
     return (e_field, h_field, summed / cells)
 

time: 370 us -> 1090 us (2.95)
  the two profiles are of different devices: /device:TPU:1 before, /device:TPU:3 now
where the time goes in v1:
time: 1090 us
  blocking collectives  837 us (77%)
  local copies, waits for them, and re-layouts  113 us (10%)
  starting transfers between devices  96.8 us (9%)
  waiting for transfers between devices  32 us (3%)
    all_gather x1, blocking collectives, render_node_over_axis(): return jnp.sum(lax.all_gather(in_array, axis_name=a_name), 0)  837 us
    ppermute x16, starting transfers between devices, from_behind(): return lax.ppermute(value, axis, pairs)  96.8 us
    mul x8, local copies, waits for them, and re-layouts, body(): filtered = filtered + weights[:, None, None, None, None] * e_field[None]  86.2 us
    ppermute x16, waiting for transfers between devices, from_behind(): return lax.ppermute(value, axis, pairs)  32 us
    mul x4, local copies, waits for them, and re-layouts, body(): weighted = (filtered * permit[None, None]).reshape(FILTERS, count, SOURCES)  22.1 us
  transfers between devices with their start and end apart: 16, of which 10 were waited for; matrix products, arithmetic and copies ran while one was open for 8% of the time, Pallas kernels for 0%

profile of v1, /device:TPU:3, one launch (start us, length us, event | category | flops | bytes accessed | tf_op | source)
XLA Modules:
  0.0 1087.1 jit_solution(1790032377414696749)
XLA Ops:
  4.2 8.5 collective-permute-start
  16.2 14.0 %mul.282 = f32[24576,2]{1,0:T(8,128)} reshape(f32[3,8,16,128]{3,2,1,0:T(8,128)S(1)} %mul.281) | data formatting | bytes 393216 | tf_op jit(solution)/shard_map/mul | solution.py:81
  30.2 7.5 copy.782
  42.0 3.7 collective-permute-done.2
  45.7 11.0 %collective-permute-done.3 = f32[2,1,16,128]{3,2,1,0:T(8,128)S(1)} collective-permute-done((f32[2,1,16,128]{3,2,1,0:T(8,128)S(1)}, f32[2,1,16,128]{3,2,1,0:T(8,128)S(1)}, u32[]{:S(2)}, u32[]{:S(2)}) %collective-permute-start.3) | collective-permute-done | bytes 16416 | tf_op jit(solution)/shard_map/ppermute | solution.py:17
  56.9 16.3 %collective-permute-start.5 = (f32[2,1,16,128]{3,2,1,0:T(8,128)S(1)}, f32[2,1,16,128]{3,2,1,0:T(8,128)S(1)}, u32[]{:S(2)}, u32[]{:S(2)}) collective-permute-start(f32[2,1,16,128]{3,2,1,0:T(8,128)S(1)} %pad_maximum_fusion.6), channel_id=1, source_target_pairs={{0,496},{16,0},{32,16},{48,32},{64,48},{80,64},{96,80},{112,96},{1... | collective-permute-start | bytes 49160 | tf_op jit(solution)/shard_map/ppermute | solution.py:17
  74.1 6.0 collective-permute-start.4
  80.3 14.0 %mul.260 = f32[24576,2]{1,0:T(8,128)} reshape(f32[3,8,16,128]{3,2,1,0:T(8,128)S(1)} %pad_maximum_fusion.1) | data formatting | bytes 393216 | tf_op jit(solution)/shard_map/mul | solution.py:79
  94.3 7.5 copy.777
  105.9 5.0 collective-permute-done.6
  111.2 14.4 %collective-permute-start.9 = (f32[2,1,16,128]{3,2,1,0:T(8,128)S(1)}, f32[2,1,16,128]{3,2,1,0:T(8,128)S(1)}, u32[]{:S(2)}, u32[]{:S(2)}) collective-permute-start(f32[2,1,16,128]{3,2,1,0:T(8,128)S(1)} %pad_maximum_fusion.5), channel_id=1, source_target_pairs={{0,496},{16,0},{32,16},{48,32},{64,48},{80,64},{96,80},{112,96},{1... | collective-permute-start | bytes 49160 | tf_op jit(solution)/shard_map/ppermute | solution.py:17
  126.4 10.0 collective-permute-start.8
  136.5 14.0 %mul.265 = f32[24576,2]{1,0:T(8,128)} reshape(f32[3,8,16,128]{3,2,1,0:T(8,128)S(1)} %pad_maximum_fusion.2) | data formatting | bytes 393216 | tf_op jit(solution)/shard_map/mul | solution.py:79
  150.5 7.5 copy.778
  162.2 5.0 collective-permute-done.10
  167.5 16.9 %collective-permute-start.13 = (f32[2,1,16,128]{3,2,1,0:T(8,128)S(1)}, f32[2,1,16,128]{3,2,1,0:T(8,128)S(1)}, u32[]{:S(2)}, u32[]{:S(2)}) collective-permute-start(f32[2,1,16,128]{3,2,1,0:T(8,128)S(1)} %pad_maximum_fusion.4), channel_id=1, source_target_pairs={{0,496},{16,0},{32,16},{48,32},{64,48},{80,64},{96,80},{112,96},{1... | collective-permute-start | bytes 49160 | tf_op jit(solution)/shard_map/ppermute | solution.py:17
  185.3 7.4 collective-permute-start.12
  192.8 14.0 %mul.271 = f32[24576,2]{1,0:T(8,128)} reshape(f32[3,8,16,128]{3,2,1,0:T(8,128)S(1)} %pad_maximum_fusion.3) | data formatting | bytes 393216 | tf_op jit(solution)/shard_map/mul | solution.py:79
  206.8 7.5 copy.779
  216.6 2.1 collective-permute-start.15
  218.7 4.8 collective-permute-done.14
  223.8 14.0 %mul.277 = f32[24576,2]{1,0:T(8,128)} reshape(f32[3,8,16,128]{3,2,1,0:T(8,128)S(1)} %pad_maximum_fusion) | data formatting | bytes 393216 | tf_op jit(solution)/shard_map/mul | solution.py:79
  237.8 7.5 copy.780
  249.3 836.6 %all-gather = f32[4096,8]{1,0:T(8,128)S(1)} all-gather(f32[8,8]{1,0:T(8,128)S(1)} %fusion.85), channel_id=2, replica_groups=mesh['gx'=32,'gy'=16] {'gx','gy'}, dimensions={0}, use_global_device_ids=true | all-gather | bytes 131328 | tf_op jit(solution)/shard_map/all_gather | solution.py:69
  (154 shorter events, 30.1 us)
Async XLA Ops:
  1.4 36.4 %collective-permute-start.1 = (f32[2,1,16,128]{3,2,1,0:T(8,128)S(1)}, f32[2,1,16,128]{3,2,1,0:T(8,128)S(1)}, u32[]{:S(2)}, u32[]{:S(2)}) collective-permute-start(f32[2,1,16,128]{3,2,1,0:T(8,128)S(1)} %slice.390), channel_id=1, source_target_pairs={{0,496},{16,0},{32,16},{48,32},{64,48},{80,64},{96,80},{112,96},{1... | collective-permute-start | bytes 49160 | tf_op jit(solution)/shard_map/ppermute | solution.py:17
  4.2 33.6 %collective-permute-start = (f32[2,8,1,128]{3,1,2,0:T(8,128)S(1)}, f32[2,8,1,128]{3,1,2,0:T(8,128)S(1)}, u32[]{:S(2)}, u32[]{:S(2)}) collective-permute-start(f32[2,8,1,128]{3,1,2,0:T(8,128)S(1)} %pad_maximum_fusion.7), channel_id=1, source_target_pairs={{0,15},{1,0},{2,1},{3,2},{4,3},{5,4},{6,5},{7,6},{8,7},{9,8},{10,9... | collective-permute-start | bytes 24584 | tf_op jit(solution)/shard_map/ppermute | solution.py:17
  16.2 21.6 %copy-start = (f32[3,8,16,128]{3,2,1,0:T(8,128)S(1)}, f32[3,8,16,128]{3,2,1,0:T(8,128)}, u32[]{:S(2)}) copy-start(f32[3,8,16,128]{3,2,1,0:T(8,128)} %param.5) | copy-start | bytes 589828
  16.2 21.8 %copy-start.2 = (f32[3,8,16,128]{3,2,1,0:T(8,128)S(1)}, f32[3,8,16,128]{3,2,1,0:T(8,128)}, u32[]{:S(2)}) copy-start(f32[3,8,16,128]{3,2,1,0:T(8,128)} %param.6) | copy-start | bytes 589828
  38.1 7.6 collective-permute-start.2
  40.1 16.6 %collective-permute-start.3 = (f32[2,1,16,128]{3,2,1,0:T(8,128)S(1)}, f32[2,1,16,128]{3,2,1,0:T(8,128)S(1)}, u32[]{:S(2)}, u32[]{:S(2)}) collective-permute-start(f32[2,1,16,128]{3,2,1,0:T(8,128)S(1)} %slice.517), channel_id=1, source_target_pairs={{0,16},{16,32},{32,48},{48,64},{64,80},{80,96},{96,112},{112,128},... | collective-permute-start | bytes 49160 | tf_op jit(solution)/shard_map/ppermute | solution.py:17
  56.9 17.2 %collective-permute-start.5 = (f32[2,1,16,128]{3,2,1,0:T(8,128)S(1)}, f32[2,1,16,128]{3,2,1,0:T(8,128)S(1)}, u32[]{:S(2)}, u32[]{:S(2)}) collective-permute-start(f32[2,1,16,128]{3,2,1,0:T(8,128)S(1)} %pad_maximum_fusion.6), channel_id=1, source_target_pairs={{0,496},{16,0},{32,16},{48,32},{64,48},{80,64},{96,80},{112,96},{1... | collective-permute-start | bytes 49160 | tf_op jit(solution)/shard_map/ppermute | solution.py:17
  74.1 27.7 %collective-permute-start.4 = (f32[2,8,1,128]{3,1,2,0:T(8,128)S(1)}, f32[2,8,1,128]{3,1,2,0:T(8,128)S(1)}, u32[]{:S(2)}, u32[]{:S(2)}) collective-permute-start(f32[2,8,1,128]{3,1,2,0:T(8,128)S(1)} %pad_maximum_fusion.9), channel_id=1, source_target_pairs={{0,15},{1,0},{2,1},{3,2},{4,3},{5,4},{6,5},{7,6},{8,7},{9,8},{10,9... | collective-permute-start | bytes 24584 | tf_op jit(solution)/shard_map/ppermute | solution.py:17
  102.0 8.9 collective-permute-start.6
  104.0 7.0 collective-permute-start.7
  111.2 15.2 %collective-permute-start.9 = (f32[2,1,16,128]{3,2,1,0:T(8,128)S(1)}, f32[2,1,16,128]{3,2,1,0:T(8,128)S(1)}, u32[]{:S(2)}, u32[]{:S(2)}) collective-permute-start(f32[2,1,16,128]{3,2,1,0:T(8,128)S(1)} %pad_maximum_fusion.5), channel_id=1, source_target_pairs={{0,496},{16,0},{32,16},{48,32},{64,48},{80,64},{96,80},{112,96},{1... | collective-permute-start | bytes 49160 | tf_op jit(solution)/shard_map/ppermute | solution.py:17
  126.4 31.6 %collective-permute-start.8 = (f32[2,8,1,128]{3,1,2,0:T(8,128)S(1)}, f32[2,8,1,128]{3,1,2,0:T(8,128)S(1)}, u32[]{:S(2)}, u32[]{:S(2)}) collective-permute-start(f32[2,8,1,128]{3,1,2,0:T(8,128)S(1)} %pad_maximum_fusion.11), channel_id=1, source_target_pairs={{0,15},{1,0},{2,1},{3,2},{4,3},{5,4},{6,5},{7,6},{8,7},{9,8},{10,9... | collective-permute-start | bytes 24584 | tf_op jit(solution)/shard_map/ppermute | solution.py:17
  158.3 8.9 collective-permute-start.10
  160.3 7.1 collective-permute-start.11
  167.5 17.7 %collective-permute-start.13 = (f32[2,1,16,128]{3,2,1,0:T(8,128)S(1)}, f32[2,1,16,128]{3,2,1,0:T(8,128)S(1)}, u32[]{:S(2)}, u32[]{:S(2)}) collective-permute-start(f32[2,1,16,128]{3,2,1,0:T(8,128)S(1)} %pad_maximum_fusion.4), channel_id=1, source_target_pairs={{0,496},{16,0},{32,16},{48,32},{64,48},{80,64},{96,80},{112,96},{1... | collective-permute-start | bytes 49160 | tf_op jit(solution)/shard_map/ppermute | solution.py:17
  185.3 29.1 %collective-permute-start.12 = (f32[2,8,1,128]{3,1,2,0:T(8,128)S(1)}, f32[2,8,1,128]{3,1,2,0:T(8,128)S(1)}, u32[]{:S(2)}, u32[]{:S(2)}) collective-permute-start(f32[2,8,1,128]{3,1,2,0:T(8,128)S(1)} %pad_maximum_fusion.13), channel_id=1, source_target_pairs={{0,15},{1,0},{2,1},{3,2},{4,3},{5,4},{6,5},{7,6},{8,7},{9,8},{10,9... | collective-permute-start | bytes 24584 | tf_op jit(solution)/shard_map/ppermute | solution.py:17
  214.5 30.9 %copy-start.1 = (f32[3,8,16,128]{3,2,1,0:T(8,128)}, f32[3,8,16,128]{3,2,1,0:T(8,128)S(1)}, u32[]{:S(2)}) copy-start(f32[3,8,16,128]{3,2,1,0:T(8,128)S(1)} %fusion.3) | copy-start | bytes 589828
  214.6 8.9 collective-permute-start.14
  216.6 7.1 collective-permute-start.15
  223.8 21.6 %copy-start.3 = (f32[3,8,16,128]{3,2,1,0:T(8,128)}, f32[3,8,16,128]{3,2,1,0:T(8,128)S(1)}, u32[]{:S(2)}) copy-start(f32[3,8,16,128]{3,2,1,0:T(8,128)S(1)} %pad_maximum_fusion) | copy-start | bytes 589828
